TPU v7x, 512 devices: a whole 4x4x16 slice. The times are simulated.
512 devices in a mesh: dp: 8 (over y, core), expert: 64 (over z, x).
Axes of the slice: x: 4, y: 4, z: 16, core: 2. Of those that a mesh axis runs over, the one named last changes fastest.
Arguments:
- activations: bfloat16 [32768, 2048], P(('dp', 'expert')), may hold values from -6 to 6
- curvature: bfloat16 [32768, 2048], P(('dp', 'expert')), may hold values from 0.099609375 to 10
- routes: int32 [32768, 8], P(('dp', 'expert')), may hold values from 0 to 63, all different within a row; in each aligned block of 64 rows (0 to 63, 64 to 127, ...) at most 9 rows name the same one
- route_gates: float32 [32768, 8], P(('dp', 'expert')), may hold values from 0.05 to 0.4
- w_gate: bfloat16 [64, 2048, 768], P('expert', 'dp'), may hold values from -0.125 to 0.125
- w_up: bfloat16 [64, 2048, 768], P('expert', 'dp'), may hold values from -0.125 to 0.125
- v_down: bfloat16 [64, 2048, 768], P('expert', 'dp'), may hold values from -0.21875 to 0.21875
Outputs:
- tangent_sum: float32 [32768, 2048], P(('dp', 'expert'))
- product_down: float32 [64, 2048, 768], P('expert', 'dp')
Inputs may be any that keep to these rules, and one draw needn't show every extreme that they name: `routes`: each token names 8 different experts. In each aligned block of 64 tokens (the tokens of one device) no expert is named by more than 9 tokens, a bound that some block reaches.
All inputs are finite; a program needn't handle non-finite values.
Results may differ from a plain program's by a relative error of at most 0.017.
Values may be sent and summed in bfloat16 or wider, within the bound.
A program may use at most 64 MiB of HBM per device.

v0:
```python
import jax
import jax.numpy as jnp
from jax import lax
from jax.sharding import PartitionSpec as P


def add_rows(arrived, piece):
    return jnp.dot(arrived, piece, preferred_element_type=jnp.float32)


def per_device(activations, curvature, routes, route_gates, w_gate, w_up, v_down):
    token_count = activations.shape[0]
    top_count = routes.shape[1]
    experts = lax.axis_size("expert")
    capacity = max(2, 9 * top_count * token_count // (8 * experts))
    chosen = (routes[:, :, None] == jnp.arange(experts, dtype=jnp.int32)).astype(jnp.int32)
    flat_pairs = chosen.reshape(token_count * top_count, experts)
    earlier = jnp.cumsum(flat_pairs, axis=0) - flat_pairs
    slots = jnp.sum(flat_pairs * earlier, axis=1).reshape(token_count, top_count)
    in_slot = (slots[:, :, None] == jnp.arange(capacity, dtype=jnp.int32)).astype(jnp.float32)
    chosen_float = chosen.astype(jnp.float32)
    placing = jnp.einsum("tke,tkc->ect", chosen_float, in_slot)
    gated_place = jnp.einsum(
        "tke,tkc->ect",
        chosen_float * route_gates[:, :, None],
        in_slot,
        precision=lax.Precision.HIGHEST,
    )
    outgoing = jnp.einsum(
        "ect,td->ecd", placing.astype(jnp.bfloat16), activations, preferred_element_type=jnp.float32
    ).astype(jnp.bfloat16)
    arrived = lax.all_to_all(outgoing, "expert", split_axis=0, concat_axis=0, tiled=True)
    row_count = experts * capacity
    arrived = arrived.reshape(row_count, activations.shape[1])

    def add_one(piece):
        return add_rows(arrived, piece)

    gate = add_one(lax.all_gather(w_gate[0], "dp", axis=0, tiled=True))
    up = add_one(lax.all_gather(w_up[0], "dp", axis=0, tiled=True))
    hidden = (jax.nn.silu(gate) * up).astype(jnp.bfloat16)
    back_rows = lax.dot_general(
        hidden,
        lax.all_gather(v_down[0], "dp", axis=0, tiled=True),
        (((1,), (1,)), ((), ())),
        preferred_element_type=jnp.float32,
    ).astype(jnp.bfloat16)
    returned = lax.all_to_all(
        back_rows.reshape(experts, capacity, -1), "expert", split_axis=0, concat_axis=0, tiled=True
    )
    tangent = jnp.einsum(
        "ect,ecd->td", gated_place, returned.astype(jnp.float32), precision=lax.Precision.HIGHEST
    )
    scaled = curvature.astype(jnp.float32) * tangent
    sending = jnp.einsum(
        "ect,td->ecd", gated_place, scaled, precision=lax.Precision.HIGHEST
    ).astype(jnp.bfloat16)
    received = lax.all_to_all(sending, "expert", split_axis=0, concat_axis=0, tiled=True).reshape(
        row_count, -1
    )
    product = lax.psum_scatter(
        lax.dot_general(
            received, hidden, (((0,), (0,)), ((), ())), preferred_element_type=jnp.float32
        ).astype(jnp.bfloat16),
        "dp",
        scatter_dimension=0,
        tiled=True,
    ).astype(jnp.float32)
    return (tangent, product[None])


def solution(mesh):
    return jax.shard_map(
        per_device,
        mesh=mesh,
        in_specs=(
            P(("dp", "expert"), None),
            P(("dp", "expert"), None),
            P(("dp", "expert"), None),
            P(("dp", "expert"), None),
            P("expert", "dp", None),
            P("expert", "dp", None),
            P("expert", "dp", None),
        ),
        out_specs=(P(("dp", "expert"), None), P("expert", "dp", None)),
        check_vma=False,
    )
```

profile of v0, /device:TPU:1, one launch (start us, length us, event | category | flops | bytes accessed | tf_op | source)
XLA Modules:
  0.0 698.5 jit_solution(8030646663125238700)
XLA Ops:
  7.2 0.0 copy-start
  7.2 0.0 all-gather.7.cloned.1.call-start
  7.2 0.7 all-gather.7.cloned.1.call-update
  7.9 0.0 all-gather.9.cloned.1.call-start
  8.0 0.7 all-gather.9.cloned.1.call-update
  8.7 0.8 copy.24
  9.4 0.1 eq.51
  9.5 0.1 eq.47
  9.6 1.2 reduce-window.6
  10.8 0.2 slice_reduce_fusion
  11.1 0.1 fusion.29
  11.2 0.1 eq.55
  11.3 0.5 fusion.16
  11.9 0.0 copy-done
  11.9 0.8 convolution_convert_fusion.2
  12.7 3.5 copy.30
  16.2 19.4 %all-to-all-start = ((bf16[64,9,2048]{2,1,0:T(8,128)(2,1)}), bf16[64,9,2048]{2,1,0:T(8,128)(2,1)}, u32[]{:S(2)}, u32[]{:S(2)}) async-start(bf16[64,9,2048]{2,1,0:T(8,128)(2,1)} %copy.30), calls=%async_computation | async-start | bytes 8388608 | tf_op jit(solution)/shard_map/all_to_all | solution.py:32
  35.6 0.0 all-gather.11.cloned.1.call-start
  35.6 0.7 all-gather.11.cloned.1.call-update
  36.3 182.9 %all-to-all-done = bf16[64,9,2048]{2,1,0:T(8,128)(2,1)} async-done(((bf16[64,9,2048]{2,1,0:T(8,128)(2,1)}), bf16[64,9,2048]{2,1,0:T(8,128)(2,1)}, u32[]{:S(2)}, u32[]{:S(2)}) %all-to-all-start) | async-done | bytes 2359328 | tf_op jit(solution)/shard_map/all_to_all | solution.py:32
  219.2 3.4 reshape.34
  222.6 0.0 all-gather.7.cloned.1.call-done
  222.6 5.1 fusion.4
  227.7 0.0 all-gather.9.cloned.1.call-done
  227.8 5.4 multiply_convert_fusion
  233.2 4.2 fusion.6
  237.4 2.8 reshape.35
  240.2 12.0 %all-to-all-start.1 = ((bf16[64,9,2048]{2,1,0:T(8,128)(2,1)}), bf16[64,9,2048]{2,1,0:T(8,128)(2,1)}, u32[]{:S(2)}, u32[]{:S(2)}) async-start(bf16[64,9,2048]{2,1,0:T(8,128)(2,1)} %reshape.35), calls=%async_computation.1 | async-start | bytes 8388608 | tf_op jit(solution)/shard_map/all_to_all | solution.py:48
  252.2 0.2 reduce-scatter.2.cloned.1.call-start
  252.5 0.0 copy-done.3
  252.5 0.1 copy.28
  252.6 0.9 convolution_bitcast_fusion
  253.5 0.0 copy-start.2
  253.5 0.2 copy.33
  253.7 182.3 %all-to-all-done.1 = bf16[64,9,2048]{2,1,0:T(8,128)(2,1)} async-done(((bf16[64,9,2048]{2,1,0:T(8,128)(2,1)}), bf16[64,9,2048]{2,1,0:T(8,128)(2,1)}, u32[]{:S(2)}, u32[]{:S(2)}) %all-to-all-start.1) | async-done | bytes 2359328 | tf_op jit(solution)/shard_map/all_to_all | solution.py:48
  435.9 5.9 fusion.11
  441.9 0.0 copy-done.2
  441.9 0.0 copy-start.1
  441.9 4.1 convolution_convert_fusion.1
  445.9 1.5 copy.34
  447.5 0.0 copy-done.1
  447.5 195.3 %all_to_all.15 = bf16[64,9,2048]{2,1,0:T(8,128)(2,1)} all-to-all(bf16[64,9,2048]{2,1,0:T(8,128)(2,1)S(1)} %copy.34), channel_id=1, replica_groups=mesh['dp'=8,'expert'=64] {'expert'}, dimensions={0} | all-to-all | bytes 4718592 | tf_op jit(solution)/shard_map/all_to_all | solution.py:58
  642.8 3.4 reshape.36
  646.2 0.0 copy-done.4
  646.2 4.1 convolution_convert_fusion
  650.3 0.0 reduce-scatter.2.cloned.1.call-update
  650.3 39.7 %reduce-scatter.2.cloned.1.call-done = bf16[256,768]{1,0:T(8,128)(2,1)} async-done(((bf16[2048,768]{1,0:T(8,128)(2,1)}), bf16[256,768]{1,0:T(8,128)(2,1)}) %reduce-scatter.2.cloned.1.call-update) | async-done | bytes 393232 | tf_op jit(solution)/shard_map/reduce_scatter | solution.py:61
  690.0 1.9 bitcast_convert_fusion
  (6 shorter events, 0.1 us)
Async XLA Ops:
  7.2 4.7 copy-start
  7.2 215.4 %all-gather.7.cloned.1.call-start = ((), (), s32[]{:S(2)}) async-start(), calls=%async_computation.5 | async-start | bytes 3538944 | tf_op jit(solution)/shard_map/all_gather | solution.py:39
  7.9 219.8 %all-gather.9.cloned.1.call-start = ((), (), s32[]{:S(2)}) async-start(), calls=%async_computation.6 | async-start | bytes 3538944 | tf_op jit(solution)/shard_map/all_gather | solution.py:40
  16.2 203.0 %all-to-all-start = ((bf16[64,9,2048]{2,1,0:T(8,128)(2,1)}), bf16[64,9,2048]{2,1,0:T(8,128)(2,1)}, u32[]{:S(2)}, u32[]{:S(2)}) async-start(bf16[64,9,2048]{2,1,0:T(8,128)(2,1)} %copy.30), calls=%async_computation | async-start | bytes 8388608 | tf_op jit(solution)/shard_map/all_to_all | solution.py:32
  35.6 197.6 %all-gather.11.cloned.1.call-start = ((), (), s32[]{:S(2)}) async-start(), calls=%async_computation.7 | async-start | bytes 3538944 | tf_op jit(solution)/shard_map/all_gather | solution.py:44
  240.2 12.3 %copy-start.3 = (f32[64,8]{0,1:T(8,128)S(1)}, f32[64,8]{0,1:T(8,128)}, u32[]{:S(2)}) copy-start(f32[64,8]{0,1:T(8,128)} %param.10) | copy-start | bytes 6148
  240.2 195.7 %all-to-all-start.1 = ((bf16[64,9,2048]{2,1,0:T(8,128)(2,1)}), bf16[64,9,2048]{2,1,0:T(8,128)(2,1)}, u32[]{:S(2)}, u32[]{:S(2)}) async-start(bf16[64,9,2048]{2,1,0:T(8,128)(2,1)} %reshape.35), calls=%async_computation.1 | async-start | bytes 8388608 | tf_op jit(solution)/shard_map/all_to_all | solution.py:48
  252.2 437.8 %reduce-scatter.2.cloned.1.call-start = ((), (), s32[]{:S(2)}) async-start(), calls=%async_computation.4 | async-start | bytes 3538944 | tf_op jit(solution)/shard_map/reduce_scatter | solution.py:61
  253.5 188.4 %copy-start.2 = (bf16[64,2048]{1,0:T(8,128)(2,1)S(1)}, bf16[64,2048]{1,0:T(8,128)(2,1)}, u32[]{:S(2)}) copy-start(bf16[64,2048]{1,0:T(8,128)(2,1)} %param.8) | copy-start | bytes 786436
  441.9 5.6 copy-start.1
  642.8 3.5 copy-start.4
Sparse Core Ops, SparseCore 0:
  10.1 41.1 all-gather.6
  53.5 35.5 all-gather.8
  91.2 35.5 all-gather.10
  650.4 39.5 reduce-scatter.1
where the time goes:
time: 700 us; the launch traced here: 698 us
  waiting for transfers between devices  407 us (58%)
  blocking collectives  195 us (28%)
  starting transfers between devices  31.7 us (5%)
  matrix products  31 us (4%)
  local copies, waits for them, and re-layouts  16.2 us (2%)
  between operations  13.9 us (2%)
    all_to_all x1, blocking collectives, per_device(): lax.all_to_all(sending, 'expert', split_axis=0, concat_axis=0, tiled=True)  195 us
    all_to_all x1, waiting for transfers between devices, per_device(): lax.all_to_all(outgoing, 'expert', split_axis=0, concat_axis=0, tiled=True)  183 us
    all_to_all x1, waiting for transfers between devices, per_device(): lax.all_to_all(back_rows.reshape(experts, capacity, -1), 'expert', split_...  182 us
    reduce_scatter x1, waiting for transfers between devices, per_device(): lax.psum_scatter(lax.dot_general(received, hidden, (((0,), (0,)), ((), ()...  39.7 us
    all_to_all x1, starting transfers between devices, per_device(): lax.all_to_all(outgoing, 'expert', split_axis=0, concat_axis=0, tiled=True)  19.4 us
  transfers between devices with their start and end apart: 6, of which 3 were waited for; matrix products, arithmetic and copies ran while one was open for 3% of the time, Pallas kernels for 0%

commit v1 on v0

v1 whole, which is shorter than its diff:
```python
import jax
import jax.numpy as jnp
from jax import lax
from jax.sharding import PartitionSpec as P

X = 4


def per_device(activations, curvature, routes, route_gates, w_gate, w_up, v_down):
    tokens, width = activations.shape
    experts = lax.axis_size("expert")
    top = routes.shape[1]
    capacity = max(2, 9 * top * tokens // (8 * experts))
    zs = experts // X
    columns = [[z * X + x for z in range(zs)] for x in range(X)]
    lines = [[z * X + x for x in range(X)] for z in range(zs)]
    my_z = lax.axis_index("expert") // X

    def gather_z(a):
        return lax.all_gather(a, "expert", axis=0, axis_index_groups=columns)

    def swap_x(rows):
        return lax.all_to_all(
            rows, "expert", split_axis=0, concat_axis=0, axis_index_groups=lines, tiled=True
        )

    full_gate = lax.all_gather(w_gate[0], "dp", axis=0, tiled=True)
    full_up = lax.all_gather(w_up[0], "dp", axis=0, tiled=True)
    full_down = lax.all_gather(v_down[0], "dp", axis=0, tiled=True)

    all_routes = gather_z(routes)
    all_gates = gather_z(route_gates)
    mine = my_z * X + jnp.arange(X, dtype=jnp.int32)
    match = all_routes[:, :, :, None] == mine
    chosen = jnp.any(match, axis=2)
    weight = jnp.sum(jnp.where(match, all_gates[:, :, :, None], 0.0), axis=2)
    count = chosen.astype(jnp.int32)
    slot = jnp.cumsum(count, axis=1) - count
    place = chosen[..., None] & (slot[..., None] == jnp.arange(capacity, dtype=jnp.int32))
    place = place.astype(jnp.float32)
    gated = place * weight[..., None]

    tokens_z = gather_z(activations)
    outgoing = jnp.einsum(
        "stxc,std->xscd", place.astype(jnp.bfloat16), tokens_z, preferred_element_type=jnp.float32
    ).astype(jnp.bfloat16)
    arrived = swap_x(outgoing).reshape(-1, width)
    gate = jnp.dot(arrived, full_gate, preferred_element_type=jnp.float32)
    up = jnp.dot(arrived, full_up, preferred_element_type=jnp.float32)
    hidden = (jax.nn.silu(gate) * up).astype(jnp.bfloat16)
    back = lax.dot_general(
        hidden, full_down, (((1,), (1,)), ((), ())), preferred_element_type=jnp.float32
    ).astype(jnp.bfloat16)
    returned = swap_x(back.reshape(X, zs, capacity, width))
    gated16 = gated.astype(jnp.bfloat16)
    partial = jnp.einsum(
        "stxc,xscd->std", gated16, returned, preferred_element_type=jnp.float32
    ).astype(jnp.bfloat16)
    tangent = lax.psum_scatter(
        partial, "expert", scatter_dimension=0, axis_index_groups=columns, tiled=False
    ).astype(jnp.float32)
    scaled = (curvature.astype(jnp.float32) * tangent).astype(jnp.bfloat16)
    scaled_z = gather_z(scaled)
    sending = jnp.einsum(
        "stxc,std->xscd", gated16, scaled_z, preferred_element_type=jnp.float32
    ).astype(jnp.bfloat16)
    received = swap_x(sending).reshape(-1, width)
    product = lax.psum_scatter(
        lax.dot_general(
            received, hidden, (((0,), (0,)), ((), ())), preferred_element_type=jnp.float32
        ).astype(jnp.bfloat16),
        "dp",
        scatter_dimension=0,
        tiled=True,
    ).astype(jnp.float32)
    return (tangent, product[None])


def solution(mesh):
    return jax.shard_map(
        per_device,
        mesh=mesh,
        in_specs=(
            P(("dp", "expert"), None),
            P(("dp", "expert"), None),
            P(("dp", "expert"), None),
            P(("dp", "expert"), None),
            P("expert", "dp", None),
            P("expert", "dp", None),
            P("expert", "dp", None),
        ),
        out_specs=(P(("dp", "expert"), None), P("expert", "dp", None)),
        check_vma=False,
    )
```

time: 700 us -> 499 us (0.71)
  waiting for transfers between devices: 407 us -> 310 us
  blocking collectives: 195 us -> 102 us
  starting transfers between devices: 31.7 us -> 4.56 us
  local copies, waits for them, and re-layouts: 16.2 us -> 25.4 us
  other arithmetic: 3.3 us -> 10.5 us
    all_to_all x2 -> x1, waiting for transfers between devices: 365 us -> 2.9 us  [swap_x(): lax.all_to_all(rows, 'expert', split_axis=0, concat_axis=0, axis_index_gr...]
    all_gather x3 -> x5, waiting for transfers between devices: 0.02 us -> 189 us  [the longest x2 117 us: gather_z(): return lax.all_gather(a, 'expert', axis=0, axis_index_groups=columns)]
    all_to_all x1 -> x2, blocking collectives: 195 us -> 46.8 us  [swap_x(): lax.all_to_all(rows, 'expert', split_axis=0, concat_axis=0, axis_index_gr...]
    reduce_scatter x0 -> x1, waiting for transfers between devices: none -> 69.2 us  [per_device(): lax.psum_scatter(partial, 'expert', scatter_dimension=0, axis_index_group...]
    all_gather x0 -> x2, blocking collectives: none -> 55.5 us  [gather_z(): return lax.all_gather(a, 'expert', axis=0, axis_index_groups=columns)]
    all_to_all x2 -> x1, starting transfers between devices: 31.4 us -> 4.1 us  [swap_x(): lax.all_to_all(rows, 'expert', split_axis=0, concat_axis=0, axis_index_gr...]
    all_to_all x0 -> x2, local copies, waits for them, and re-layouts: none -> 7.11 us  [swap_x(): lax.all_to_all(rows, 'expert', split_axis=0, concat_axis=0, axis_index_gr...]
    reshape x3 -> x4, local copies, waits for them, and re-layouts: 9.63 us -> 14.7 us  [the longest x2 7.93 us: per_device(): returned = swap_x(back.reshape(X, zs, capacity, width))]
  transfers between devices with their start and end apart: 6 -> 8, of which waited for: 3 -> 8; matrix products, arithmetic and copies ran while one was open for 3% -> 6% of each run, Pallas kernels for 0% -> 0%
where the time goes in v1:
time: 499 us; the launch traced here: 497 us
  waiting for transfers between devices  310 us (62%)
  blocking collectives  102 us (20%)
  matrix products  30 us (6%)
  local copies, waits for them, and re-layouts  25.4 us (5%)
  between operations  14.2 us (3%)
  other arithmetic  10.5 us (2%)
    all_gather x2, waiting for transfers between devices, gather_z(): return lax.all_gather(a, 'expert', axis=0, axis_index_groups=columns)  117 us
    reduce_scatter x1, waiting for transfers between devices, per_device(): lax.psum_scatter(partial, 'expert', scatter_dimension=0, axis_index_group...  69.2 us
    all_gather x2, blocking collectives, gather_z(): return lax.all_gather(a, 'expert', axis=0, axis_index_groups=columns)  55.5 us
    all_to_all x2, blocking collectives, swap_x(): lax.all_to_all(rows, 'expert', split_axis=0, concat_axis=0, axis_index_gr...  46.8 us
    reduce_scatter x1, waiting for transfers between devices, per_device(): lax.psum_scatter(lax.dot_general(received, hidden, (((0,), (0,)), ((), ()...  46.2 us
    all_gather x1, waiting for transfers between devices, per_device(): full_down = lax.all_gather(v_down[0], 'dp', axis=0, tiled=True)  33 us
    all_gather x1, waiting for transfers between devices, per_device(): full_up = lax.all_gather(w_up[0], 'dp', axis=0, tiled=True)  32.6 us
  transfers between devices with their start and end apart: 8, of which 8 were waited for; matrix products, arithmetic and copies ran while one was open for 6% of the time, Pallas kernels for 0%

profile of v1, /device:TPU:1, one launch (start us, length us, event | category | flops | bytes accessed | tf_op | source)
XLA Modules:
  0.0 497.1 jit_solution(8676723055005693537)
XLA Ops:
  7.2 0.0 all-gather.15.cloned.1.call-start
  7.2 0.7 all-gather.15.cloned.1.call-update
  7.9 0.0 all-gather.17.cloned.1.call-start
  7.9 0.7 all-gather.17.cloned.1.call-update
  8.6 0.0 all-gather.19.cloned.1.call-start
  8.7 0.7 all-gather.19.cloned.1.call-update
  9.4 0.0 all-gather.21.cloned.1.call-start
  9.4 0.5 all-gather.21.cloned.1.call-update
  10.0 29.8 %all-gather.7 = s32[16,64,8]{1,2,0:T(8,128)S(1)} all-gather(s32[1,64,8]{1,2,0:T(8,128)} %bitcast.49), channel_id=2, replica_groups={{0,4,8,12,16,20,24,28,32,36,40,44,48,52,56,60},{1,5,9,13,17,21,25,29,33..., dimensions={0}, use_global_device_ids=true | all-gather | bytes 34816 | tf_op jit(solution)/shard_map/all_gather | solution.py:20
  39.8 0.2 compare_reduce_fusion
  40.0 0.3 copy.41
  40.3 6.3 %fusion.27 = s32[16,64,4]{2,0,1:T(8,128)S(1)} fusion(s32[16,64,4]{2,0,1:T(8,128)S(1)} %copy.41), kind=kOutput, calls=%fused_computation.38 | output fusion | flops 258048 | bytes 32768 | tf_op jit(solution)/shard_map/jit(cumsum)/reduce_window_sum | solution.py:38
  46.6 0.3 copy.42
  46.9 38.5 %all-gather.15.cloned.1.call-done = bf16[1024,2048]{1,0:T(8,128)(2,1)} async-done(((bf16[64,2048]{1,0:T(8,128)(2,1)}), bf16[1024,2048]{1,0:T(8,128)(2,1)}) %all-gather.15.cloned.1.call-update) | async-done | bytes 4194320 | tf_op jit(solution)/shard_map/all_gather | solution.py:20
  85.4 3.4 convert_bitcast_fusion.1
  88.9 1.5 copy.44
  90.4 24.0 %all_to_all.15 = bf16[4,16,9,2048]{3,1,2,0:T(8,128)(2,1)S(1)} all-to-all(bf16[4,16,9,2048]{3,1,2,0:T(8,128)(2,1)S(1)} %copy.44), channel_id=1, replica_groups={{0,1,2,3},{4,5,6,7},{8,9,10,11},{12,13,14,15},{16,17,18,19},{20,21,22,2..., dimensions={0} | all-to-all | bytes 4718592 | tf_op jit(solution)/shard_map/all_to_all | solution.py:23
  114.4 3.6 copy.45
  117.9 3.4 reshape.35
  121.4 6.7 %all-gather.17.cloned.1.call-done = bf16[1,2048,768]{2,1,0:T(8,128)(2,1)} async-done(((bf16[1,256,768]{2,1,0:T(8,128)(2,1)}), bf16[1,2048,768]{2,1,0:T(8,128)(2,1)}) %all-gather.17.cloned.1.call-update) | async-done | bytes 3145744 | tf_op jit(solution)/shard_map/all_gather | solution.py:27
  128.1 5.1 %fusion.5 = f32[576,768]{1,0:T(8,128)} fusion(bf16[576,2048]{1,0:T(8,128)(2,1)S(1)} %reshape.35, bf16[1,2048,768]{2,1,0:T(8,128)(2,1)} %all-gather.17.cloned.1.call-done), kind=kOutput, calls=%fused_computation.9 | convolution fusion | flops 1811939328 | bytes 7274496 | tf_op jit(solution)/shard_map/dot_general | solution.py:48
  133.2 32.6 %all-gather.19.cloned.1.call-done = bf16[1,2048,768]{2,1,0:T(8,128)(2,1)} async-done(((bf16[1,256,768]{2,1,0:T(8,128)(2,1)}), bf16[1,2048,768]{2,1,0:T(8,128)(2,1)}) %all-gather.19.cloned.1.call-update) | async-done | bytes 3145744 | tf_op jit(solution)/shard_map/all_gather | solution.py:28
  165.8 4.5 multiply_convert_fusion
  170.3 33.0 %all-gather.21.cloned.1.call-done = bf16[1,2048,768]{2,1,0:T(8,128)(2,1)} async-done(((bf16[1,256,768]{2,1,0:T(8,128)(2,1)}), bf16[1,2048,768]{2,1,0:T(8,128)(2,1)}) %all-gather.21.cloned.1.call-update) | async-done | bytes 3145744 | tf_op jit(solution)/shard_map/all_gather | solution.py:29
  203.4 3.9 fusion.7
  207.3 2.8 reshape.36
  210.1 5.1 %copy.46 = bf16[4,16,9,2048]{3,1,2,0:T(8,128)(2,1)} copy(bf16[4,16,9,2048]{3,2,1,0:T(8,128)(2,1)} %reshape.36) | data formatting | bytes 4718592 | tf_op jit(solution)/shard_map/reshape | solution.py:54
  215.2 4.1 all-to-all-start.1
  219.3 25.6 %all-gather.8 = f32[16,64,8]{1,2,0:T(8,128)S(1)} all-gather(f32[1,64,8]{1,2,0:T(8,128)S(1)} %bitcast.50), channel_id=3, replica_groups={{0,4,8,12,16,20,24,28,32,36,40,44,48,52,56,60},{1,5,9,13,17,21,25,29,33..., dimensions={0}, use_global_device_ids=true | all-gather | bytes 34816 | tf_op jit(solution)/shard_map/all_gather | solution.py:20
  245.0 0.2 fusion.13
  245.1 2.9 all-to-all-done.1
  248.0 5.6 %bitcast_convert_fusion = bf16[16,64,2048]{2,1,0:T(8,128)(2,1)} fusion(bf16[4,16,9,2048]{3,1,2,0:T(8,128)(2,1)S(1)} %all-to-all-done.1, bf16[16,64,4]{1,2,0:T(4,128)(2,1)S(1)} %fusion.13, s32[16,64,4]{1,2,0:T(4,128)S(1)} %copy.43, pred[16,64,4]{1,2,0:T(4,128)(4,1)S(1)} %compare_reduce_fusion), kind=kOutput, calls=%fused_computation | convolution fusion | flops 153202688 | bytes 6582272 | tf_op jit(solution)/shard_map/stxc,xscd->std/dot_general | solution.py:56
  253.6 0.0 reduce-scatter.3.cloned.1.call-update
  253.7 0.0 all-gather.23.cloned.1.call-start
  253.7 69.2 %reduce-scatter.3.cloned.1.call-done = bf16[1,64,2048]{2,1,0:T(8,128)(2,1)} async-done(((bf16[16,64,2048]{2,1,0:T(8,128)(2,1)}), bf16[1,64,2048]{2,1,0:T(8,128)(2,1)}) %reduce-scatter.3.cloned.1.call-update) | async-done | bytes 262160 | tf_op jit(solution)/shard_map/reduce_scatter | solution.py:59
  322.9 1.9 multiply_convert_fusion.1
  324.8 0.0 all-gather.23.cloned.1.call-update
  324.8 0.3 reduce-scatter.5.cloned.1.call-start
  325.1 78.4 %all-gather.23.cloned.1.call-done = bf16[1024,2048]{1,0:T(8,128)(2,1)} async-done(((bf16[64,2048]{1,0:T(8,128)(2,1)}), bf16[1024,2048]{1,0:T(8,128)(2,1)}) %all-gather.23.cloned.1.call-update) | async-done | bytes 4194320 | tf_op jit(solution)/shard_map/all_gather | solution.py:20
  403.4 3.4 convert_bitcast_fusion
  406.9 1.4 copy.48
  408.3 22.8 %all_to_all.16 = bf16[4,16,9,2048]{3,1,2,0:T(8,128)(2,1)S(1)} all-to-all(bf16[4,16,9,2048]{3,1,2,0:T(8,128)(2,1)S(1)} %copy.48), channel_id=1, replica_groups={{0,1,2,3},{4,5,6,7},{8,9,10,11},{12,13,14,15},{16,17,18,19},{20,21,22,2..., dimensions={0} | all-to-all | bytes 4718592 | tf_op jit(solution)/shard_map/all_to_all | solution.py:23
  431.1 3.5 copy.49
  434.7 3.4 reshape.37
  438.0 4.1 convolution_convert_fusion
  442.1 0.0 reduce-scatter.5.cloned.1.call-update
  442.1 46.2 %reduce-scatter.5.cloned.1.call-done = bf16[256,768]{1,0:T(8,128)(2,1)} async-done(((bf16[2048,768]{1,0:T(8,128)(2,1)}), bf16[256,768]{1,0:T(8,128)(2,1)}) %reduce-scatter.5.cloned.1.call-update) | async-done | bytes 393232 | tf_op jit(solution)/shard_map/reduce_scatter | solution.py:68
  488.3 1.9 bitcast_convert_fusion.1
  (9 shorter events, 0.0 us)
Async XLA Ops:
  7.2 78.3 %all-gather.15.cloned.1.call-start = ((), (), s32[]{:S(2)}) async-start(), calls=%async_computation.7 | async-start | bytes 4456448 | tf_op jit(solution)/shard_map/all_gather | solution.py:20
  7.9 120.2 %all-gather.17.cloned.1.call-start = ((), (), s32[]{:S(2)}) async-start(), calls=%async_computation.8 | async-start | bytes 3538944 | tf_op jit(solution)/shard_map/all_gather | solution.py:27
  8.6 157.2 %all-gather.19.cloned.1.call-start = ((), (), s32[]{:S(2)}) async-start(), calls=%async_computation.9 | async-start | bytes 3538944 | tf_op jit(solution)/shard_map/all_gather | solution.py:28
  9.4 194.0 %all-gather.21.cloned.1.call-start = ((), (), s32[]{:S(2)}) async-start(), calls=%async_computation.10 | async-start | bytes 3538944 | tf_op jit(solution)/shard_map/all_gather | solution.py:29
  215.2 4.1 copy-start.1
  215.2 32.8 %all-to-all-start.1 = ((bf16[4,16,9,2048]{3,1,2,0:T(8,128)(2,1)}), bf16[4,16,9,2048]{3,1,2,0:T(8,128)(2,1)S(1)}, u32[]{:S(2)}, u32[]{:S(2)}) async-start(bf16[4,16,9,2048]{3,1,2,0:T(8,128)(2,1)} %copy.46), calls=%async_computation.1 | async-start | bytes 4718592 | tf_op jit(solution)/shard_map/all_to_all | solution.py:23
  219.3 103.5 %reduce-scatter.3.cloned.1.call-start = ((), (), s32[]{:S(2)}) async-start(), calls=%async_computation.5 | async-start | bytes 4456448 | tf_op jit(solution)/shard_map/reduce_scatter | solution.py:59
  253.6 69.2 %copy-start = (bf16[64,2048]{1,0:T(8,128)(2,1)S(1)}, bf16[64,2048]{1,0:T(8,128)(2,1)}, u32[]{:S(2)}) copy-start(bf16[64,2048]{1,0:T(8,128)(2,1)} %param.8) | copy-start | bytes 786436
  253.7 149.8 %all-gather.23.cloned.1.call-start = ((), (), s32[]{:S(2)}) async-start(), calls=%async_computation.11 | async-start | bytes 4456448 | tf_op jit(solution)/shard_map/all_gather | solution.py:20
  324.8 163.5 %reduce-scatter.5.cloned.1.call-start = ((), (), s32[]{:S(2)}) async-start(), calls=%async_computation.6 | async-start | bytes 3538944 | tf_op jit(solution)/shard_map/reduce_scatter | solution.py:68
Sparse Core Ops, SparseCore 0:
  10.1 75.3 all-gather.14
  87.5 40.5 all-gather.16
  130.2 35.5 all-gather.18
  167.8 35.5 all-gather.20
  253.8 69.0 reduce-scatter.2
  325.4 78.0 all-gather.22
  442.3 46.0 reduce-scatter.4

commit v2 on v0

v2 whole, which is shorter than its diff:
```python
import functools

import jax
import jax.numpy as jnp
from jax import lax
from jax.experimental import pallas as pl
from jax.experimental.pallas import tpu as pltpu
from jax.sharding import PartitionSpec as P

X = 4
Y = 4
HALF = 8
TOK = 64
CAP = 9
CHUNKS = 4
PAIR = 2 * TOK
GROUPS = ((1, 2, 3), (4, 5, 6), (7, 0))
ROWS = tuple(-(-len(g) * 2 * CAP // 16) * 16 for g in GROUPS)
STARTS = tuple(X * sum(ROWS[:g]) for g in range(len(GROUPS)))
TOTAL = X * sum(ROWS)
LAG = 1
MESH = pl.DeviceIdType.MESH
F32 = jnp.float32
BF16 = jnp.bfloat16


def dot(a, b, dims=((1,), (0,))):
    return lax.dot_general(a, b, (dims, ((), ())), preferred_element_type=F32)


def kernel(
    tok_ref, curv_ref, tab_ref, wg_ref, wu_ref, wd_ref, tan_ref, out_ref,
    wf, zb1, tb, qs, ws, pm0, pm1, pm2, gm0, gm1, gm2, gt0, gt1, gt2,
    st1, arr, hid, st2, br, rs_s, rs_r, sc, zb3, st3, rr, own, ps, pr, ys, yr,
    w_loc, w_ss, w_rs, f_ss, f_rs, z1_s, z1_r, t_s, t_r, x1_s, x1_r, x2_s, x2_r,
    rs_ss, rs_rs, z3_s, z3_r, x3_s, x3_r, p_s, p_r, y_s, y_r,
):
    pm, gm, gt = (pm0, pm1, pm2), (gm0, gm1, gm2), (gt0, gt1, gt2)
    dp = lax.axis_index("dp")
    e = lax.axis_index("expert")
    zi, xi = e // X, lax.rem(e, X)
    yi, ci = dp // 2, lax.rem(dp, 2)
    width = tok_ref.shape[1]
    cw = width // CHUNKS
    drows = wg_ref.shape[0]
    experts = 4 * HALF * 2

    def at_z(step):
        return (dp, lax.rem(e + step * X + experts, experts))

    def at_x(step):
        return (dp, zi * X + lax.rem(xi + step + X, X))

    def at_y(step):
        return (lax.rem(yi + step + Y, Y) * 2 + ci, e)

    sibling = (yi * 2 + (1 - ci), e)
    sends = []

    def remote(src, dst, ss, rs, dev):
        return pltpu.make_async_remote_copy(
            src_ref=src, dst_ref=dst, send_sem=ss, recv_sem=rs, device_id=dev, device_id_type=MESH
        )

    def go(copy):
        copy.start()
        sends.append(copy)

    barrier = pltpu.get_barrier_semaphore()
    partners = [at_z(1), at_z(-1), at_x(1), at_x(2), at_x(3), at_y(1), at_y(2), at_y(3), sibling]
    for dev in partners:
        pl.semaphore_signal(barrier, inc=1, device_id=dev, device_id_type=MESH)
    pl.semaphore_wait(barrier, len(partners))

    def z1_copy(d, k, j):
        src = tok_ref.at[:, j * cw : (j + 1) * cw] if k == 0 else zb1.at[d, k - 1, j]
        return remote(src, zb1.at[d, k, j], z1_s.at[d, k, j], z1_r.at[d, k, j], at_z(1 - 2 * d))

    def t_copy(d, k):
        src = tab_ref if k == 0 else tb.at[d, k - 1]
        return remote(src, tb.at[d, k], t_s.at[d, k], t_r.at[d, k], at_z(1 - 2 * d))

    def z3_copy(d, k, i):
        src = sc.at[i] if k == 0 else zb3.at[d, k - 1, i]
        return remote(src, zb3.at[d, k, i], z3_s.at[d, k, i], z3_r.at[d, k, i], at_z(1 - 2 * d))

    def rs_copy(d, s, i):
        return remote(
            rs_s.at[d, s, i], rs_r.at[d, s, i], rs_ss.at[d, s, i], rs_rs.at[d, s, i], at_z(1 - 2 * d)
        )

    def live(d, k, j):
        return k < HALF - 1 or (j < CHUNKS // 2) == (d == 0)

    def block(g, r):
        return slice(STARTS[g] + r * ROWS[g], STARTS[g] + (r + 1) * ROWS[g])

    def group(g):
        return slice(STARTS[g], STARTS[g] + X * ROWS[g])

    def x1_copy(g, r):
        rows = block(g, r)
        return remote(st1.at[rows], arr.at[rows], x1_s.at[g, r], x1_r.at[g, r], at_x(r))

    def x2_copy(g, i, r):
        rows = block(g, r)
        return remote(
            st2.at[i, rows], br.at[i, rows], x2_s.at[g, i, r], x2_r.at[g, i, r], at_x(-r)
        )

    def x3_copy(g, i, r):
        rows = block(g, r)
        return remote(st3.at[i, rows], rr.at[i, rows], x3_s.at[g, i, r], x3_r.at[g, i, r], at_x(r))

    def wrows(y):
        return pl.ds(pl.multiple_of((y * 2 + ci) * drows, drows), drows)

    w_refs = (wg_ref, wu_ref, wd_ref)

    def w_copy(m, r):
        return remote(
            w_refs[m], wf.at[m, wrows(yi)], w_ss.at[m, r - 1], w_rs.at[m, r - 1], at_y(r)
        )

    def f_copy(m, r):
        if r == 0:
            return remote(w_refs[m], wf.at[m, wrows(yi)], f_ss.at[m, r], f_rs.at[m, r], sibling)
        rows = wrows(lax.rem(yi - r + Y, Y))
        return remote(wf.at[m, rows], wf.at[m, rows], f_ss.at[m, r], f_rs.at[m, r], sibling)

    def w_local(m):
        return pltpu.make_async_copy(w_refs[m], wf.at[m, wrows(yi)], w_loc.at[m])

    def share_weight(m):
        for r in (1, 3, 2):
            w_copy(m, r).wait_recv()
            go(f_copy(m, r))

    def finish_weight(m):
        w_local(m).wait()
        for r in range(Y):
            f_copy(m, r).wait_recv()

    lane = lax.broadcasted_iota(jnp.int32, (1, PAIR), 1)
    upper_row = lax.broadcasted_iota(jnp.int32, (PAIR, PAIR), 0)
    upper_col = lax.broadcasted_iota(jnp.int32, (PAIR, PAIR), 1)
    before = (upper_row < upper_col) & ((upper_row < TOK) == (upper_col < TOK))
    before = before.astype(F32).astype(BF16)

    def route(k, spot):
        if k == 0:
            first, second = tab_ref[...], tb[0, HALF - 1]
        else:
            first, second = tb[0, k - 1], tb[1, k - 1]
        table = jnp.where(lane < TOK, first, second)
        gates, names = table[:8], table[8:]
        count, weight = [], []
        for r in range(X):
            expert = (zi * X + lax.rem(xi + r, X)).astype(F32)
            match = names == expert
            count.append(jnp.sum(jnp.where(match, 1.0, 0.0), axis=0, keepdims=True))
            weight.append(jnp.sum(jnp.where(match, gates, 0.0), axis=0, keepdims=True))
        fill = jnp.zeros((8 - X, PAIR), F32)
        count = jnp.concatenate(count + [fill], axis=0)
        slot = dot(count.astype(BF16), before)
        base = jnp.where(lane < TOK, 2 * CAP * spot, 2 * CAP * spot + CAP).astype(F32)
        qs[k] = jnp.where(count > 0.0, slot + base, -1.0)
        ws[k] = jnp.concatenate(weight + [fill], axis=0)

    def tables(g):
        rows = ROWS[g]
        for spot, k in enumerate(GROUPS[g]):
            cols = slice(spot * PAIR, (spot + 1) * PAIR)
            number = lax.broadcasted_iota(jnp.int32, (rows, PAIR), 0).astype(F32)
            parts = []
            for r in range(X):
                hit = number == qs[k][r : r + 1]
                here = slice(r * rows, (r + 1) * rows)
                pm[g][here, cols] = jnp.where(hit, 1.0, 0.0).astype(BF16)
                weighted = jnp.where(hit, ws[k][r : r + 1], 0.0)
                gm[g][here, cols] = weighted.astype(BF16)
                parts.append(weighted)
            gt[g][cols, :] = jnp.concatenate(parts, axis=0).T.astype(BF16)

    def tokens_of(k, j):
        cols = slice(j * cw, (j + 1) * cw)
        if k == 0:
            return [tok_ref[:, cols], zb1[0 if j < CHUNKS // 2 else 1, HALF - 1, j]]
        return [zb1[0, k - 1, j], zb1[1, k - 1, j]]

    def select(g):
        for j in range(CHUNKS):
            cols = slice(j * cw, (j + 1) * cw)
            source = jnp.concatenate([t for k in GROUPS[g] for t in tokens_of(k, j)], axis=0)
            picked = dot(pm[g][...], source).astype(BF16)
            arr[block(g, 0), cols] = picked[: ROWS[g]]
            st1[STARTS[g] + ROWS[g] : STARTS[g] + X * ROWS[g], cols] = picked[ROWS[g] :]
        for r in (2, 1, 3):
            go(x1_copy(g, r))

    def hide(g):
        for r in (2, 1, 3):
            x1_copy(g, r).wait_recv()

        def tile(n, _):
            cols = pl.ds(pl.multiple_of(n * 256, 256), 256)
            gate = dot(arr[group(g), :], wf[0, :, cols])
            up = dot(arr[group(g), :], wf[1, :, cols])
            hid[group(g), cols] = (gate / (1.0 + jnp.exp(-gate)) * up).astype(BF16)
            return 0

        lax.fori_loop(0, hid.shape[1] // 256, tile, 0)

    for m in range(3):
        w_local(m).start()
    for j in range(CHUNKS):
        for d in range(2):
            if j == 0:
                go(t_copy(d, 0))
            go(z1_copy(d, 0, j))
    for m in range(3):
        for r in (1, 3, 2):
            go(w_copy(m, r))
        go(f_copy(m, 0))

    for k in range(1, HALF + 1):
        for j in range(CHUNKS):
            for d in range(2):
                if j == 0 and (k < HALF or d == 0):
                    t_copy(d, k - 1).wait_recv()
                    if k < HALF - 1 or (k == HALF - 1 and d == 0):
                        go(t_copy(d, k))
                if live(d, k - 1, j):
                    z1_copy(d, k - 1, j).wait_recv()
                if k < HALF and live(d, k, j):
                    go(z1_copy(d, k, j))
        pair = k % HALF
        for g, members in enumerate(GROUPS):
            if pair in members:
                route(pair, members.index(pair))
                if pair == members[-1]:
                    tables(g)
                    select(g)
        if k == 4:
            share_weight(0)
        if k == 7:
            share_weight(1)
            finish_weight(0)
            finish_weight(1)
            hide(0)
    hide(1)
    share_weight(2)
    hide(2)
    finish_weight(2)

    def place(i):
        return lax.rem(yi + 1 + i, CHUNKS)

    def back(g, i):
        rows = pl.ds(pl.multiple_of(place(i) * cw, cw), cw)
        made = dot(hid[group(g), :], wf[2, rows, :], ((1,), (1,))).astype(BF16)
        br[i, block(g, 0)] = made[: ROWS[g]]
        st2[i, STARTS[g] + ROWS[g] : STARTS[g] + X * ROWS[g]] = made[ROWS[g] :]
        for r in (2, 1, 3):
            go(x2_copy(g, i, r))

    def share(k, i):
        for g, members in enumerate(GROUPS):
            if k in members:
                spot = members.index(k)
                return dot(gt[g][spot * PAIR : (spot + 1) * PAIR, :], br[i, group(g)])

    order = len(GROUPS) - 1

    def reduce_step(i, s):
        if s in (0, 2, 5):
            g = {0: 2, 2: 1, 5: 0}[s]
            for r in (2, 1, 3):
                x2_copy(g, i, r).wait_recv()
        part = share((HALF - s) % HALF, i)
        if s == 0:
            d = 0 if i < CHUNKS // 2 else 1
            rs_s[d, 0, i] = part[TOK:].astype(BF16)
            go(rs_copy(d, 0, i))
            own[i] = part[:TOK]
            back(1, i)
        else:
            for d in range(2):
                mine = part[TOK:] if d == 0 else part[:TOK]
                if s > 1 or live(d, HALF - 1, i):
                    rs_copy(d, s - 1, i).wait_recv()
                    mine = mine + rs_r[d, s - 1, i].astype(F32)
                rs_s[d, s, i] = mine.astype(BF16)
                go(rs_copy(d, s, i))
            if s == 1:
                back(0, i)

    def finish_tangent(i):
        cols = pl.ds(pl.multiple_of(place(i) * cw, cw), cw)
        total = own[i]
        for d in range(2):
            rs_copy(d, HALF - 1, i).wait_recv()
            total = total + rs_r[d, HALF - 1, i].astype(F32)
        tan_ref[:, cols] = total
        sc[i] = (curv_ref[:, cols].astype(F32) * total).astype(BF16)
        for d in range(2):
            go(z3_copy(d, 0, i))

    def scaled_of(k, i):
        if k == 0:
            return [sc[i], zb3[0 if i < CHUNKS // 2 else 1, HALF - 1, i]]
        return [zb3[0, k - 1, i], zb3[1, k - 1, i]]

    def gather_step(i, k):
        for d in range(2):
            if live(d, k - 1, i):
                z3_copy(d, k - 1, i).wait_recv()
            if k < HALF and live(d, k, i):
                go(z3_copy(d, k, i))
        for g, members in enumerate(GROUPS):
            if k % HALF == members[-1]:
                source = jnp.concatenate([t for m in members for t in scaled_of(m, i)], axis=0)
                picked = dot(gm[g][...], source).astype(BF16)
                rr[i, block(g, 0)] = picked[: ROWS[g]]
                st3[i, STARTS[g] + ROWS[g] : STARTS[g] + X * ROWS[g]] = picked[ROWS[g] :]
                for r in (2, 1, 3):
                    go(x3_copy(g, i, r))

    hw = cw // 2
    held = []

    def multiply(i):
        for g in range(len(GROUPS)):
            for r in (2, 1, 3):
                x3_copy(g, i, r).wait_recv()
        theirs = pl.ds(pl.multiple_of((1 - ci) * hw, hw), hw)
        mine = pl.ds(pl.multiple_of(ci * hw, hw), hw)
        ps[i] = dot(rr[i, :, theirs], hid[...], ((0,), (0,))).astype(BF16)
        go(remote(ps.at[i], pr.at[i], p_s.at[i], p_r.at[i], sibling))
        out_ref[...] = dot(rr[i, :, mine], hid[...], ((0,), (0,)))
        remote(ps.at[i], pr.at[i], p_s.at[i], p_r.at[i], sibling).wait_recv()
        total = out_ref[...] + pr[i].astype(F32)
        if i < Y - 1:
            ys[i] = total.astype(BF16)
            go(remote(ys.at[i], yr.at[i], y_s.at[i], y_r.at[i], at_y(1 + i)))
        else:
            for n in range(Y - 1):
                remote(ys.at[n], yr.at[n], y_s.at[n], y_r.at[n], at_y(1 + n)).wait_recv()
                total = total + yr[n].astype(F32)
            out_ref[...] = total

    for i in range(CHUNKS):
        back(2, i)
    for tick in range(2 * HALF + 2 + LAG * (CHUNKS - 1)):
        for i in range(CHUNKS):
            u = tick - LAG * i
            if 0 <= u < HALF:
                reduce_step(i, u)
            elif u == HALF:
                finish_tangent(i)
            elif HALF < u <= 2 * HALF:
                gather_step(i, u - HALF)
            elif u == 2 * HALF + 1:
                multiply(i)

    for copy in sends:
        copy.wait_send()


def per_device(activations, curvature, routes, route_gates, w_gate, w_up, v_down):
    tokens, width = activations.shape
    features, hidden = w_gate.shape[1:]
    cw = width // CHUNKS
    table = jnp.concatenate([route_gates.T, routes.T.astype(F32)], axis=0)
    table = jnp.concatenate([table, table], axis=1)
    vmem = pl.BlockSpec(memory_space=pltpu.VMEM)
    hbm = pl.BlockSpec(memory_space=pl.ANY)
    dma = pltpu.SemaphoreType.DMA
    n = len(GROUPS)
    scratch = [
        pltpu.VMEM((3, width, hidden), BF16),
        pltpu.VMEM((2, HALF, CHUNKS, tokens, cw), BF16),
        pltpu.VMEM((2, HALF) + table.shape, F32),
        pltpu.VMEM((HALF, 8, PAIR), F32),
        pltpu.VMEM((HALF, 8, PAIR), F32),
    ]
    scratch += [pltpu.VMEM((X * ROWS[g], PAIR * len(GROUPS[g])), BF16) for g in range(n)] * 2
    scratch += [pltpu.VMEM((PAIR * len(GROUPS[g]), X * ROWS[g]), BF16) for g in range(n)]
    scratch += [
        pltpu.VMEM((TOTAL, width), BF16),
        pltpu.VMEM((TOTAL, width), BF16),
        pltpu.VMEM((TOTAL, hidden), BF16),
        pltpu.VMEM((CHUNKS, TOTAL, cw), BF16),
        pltpu.VMEM((CHUNKS, TOTAL, cw), BF16),
        pltpu.VMEM((2, HALF, CHUNKS, tokens, cw), BF16),
        pltpu.VMEM((2, HALF, CHUNKS, tokens, cw), BF16),
        pltpu.VMEM((CHUNKS, tokens, cw), BF16),
        pltpu.VMEM((2, HALF, CHUNKS, tokens, cw), BF16),
        pltpu.VMEM((CHUNKS, TOTAL, cw), BF16),
        pltpu.VMEM((CHUNKS, TOTAL, cw), BF16),
        pltpu.VMEM((CHUNKS, tokens, cw), F32),
        pltpu.VMEM((CHUNKS, features, hidden), BF16),
        pltpu.VMEM((CHUNKS, features, hidden), BF16),
        pltpu.VMEM((Y - 1, features, hidden), BF16),
        pltpu.VMEM((Y - 1, features, hidden), BF16),
        dma((3,)),
        dma((3, Y - 1)), dma((3, Y - 1)),
        dma((3, Y)), dma((3, Y)),
        dma((2, HALF, CHUNKS)), dma((2, HALF, CHUNKS)),
        dma((2, HALF)), dma((2, HALF)),
        dma((n, X)), dma((n, X)),
        dma((n, CHUNKS, X)), dma((n, CHUNKS, X)),
        dma((2, HALF, CHUNKS)), dma((2, HALF, CHUNKS)),
        dma((2, HALF, CHUNKS)), dma((2, HALF, CHUNKS)),
        dma((n, CHUNKS, X)), dma((n, CHUNKS, X)),
        dma((CHUNKS,)), dma((CHUNKS,)),
        dma((Y - 1,)), dma((Y - 1,)),
    ]
    tangent, product = pl.pallas_call(
        kernel,
        out_shape=(
            jax.ShapeDtypeStruct((tokens, width), F32),
            jax.ShapeDtypeStruct((features, hidden), F32),
        ),
        in_specs=[vmem, vmem, vmem, hbm, hbm, hbm],
        out_specs=(vmem, vmem),
        scratch_shapes=scratch,
        compiler_params=pltpu.CompilerParams(
            collective_id=0, has_side_effects=True, vmem_limit_bytes=62 * 2**20
        ),
    )(activations, curvature, table, w_gate[0], w_up[0], v_down[0])
    return (tangent, product[None])


def solution(mesh):
    return jax.shard_map(
        per_device,
        mesh=mesh,
        in_specs=(
            P(("dp", "expert"), None),
            P(("dp", "expert"), None),
            P(("dp", "expert"), None),
            P(("dp", "expert"), None),
            P("expert", "dp", None),
            P("expert", "dp", None),
            P("expert", "dp", None),
        ),
        out_specs=(P(("dp", "expert"), None), P("expert", "dp", None)),
        check_vma=False,
    )
```

time: 700 us -> 211 us (0.30)
  waiting for transfers between devices: 407 us -> 0 us
  Pallas kernels: 0 us -> 205 us
  blocking collectives: 195 us -> 0 us
  starting transfers between devices: 31.7 us -> 0 us
  matrix products: 31 us -> 0 us
  between operations: 13.9 us -> 0.66 us
  local copies, waits for them, and re-layouts: 16.2 us -> 4.19 us
    all_to_all x2 -> x0, waiting for transfers between devices: 365 us -> none  [the longest x1 183 us: per_device(): lax.all_to_all(outgoing, 'expert', split_axis=0, concat_axis=0, tiled=True)]
    pallas_call x0 -> x1, Pallas kernels: none -> 205 us  [per_device(): pl.pallas_call(kernel, out_shape=(jax.ShapeDtypeStruct((tokens, width), F...]
    all_to_all x1 -> x0, blocking collectives: 195 us -> none  [per_device(): lax.all_to_all(sending, 'expert', split_axis=0, concat_axis=0, tiled=True)]
    reduce_scatter x1 -> x0, waiting for transfers between devices: 39.7 us -> none  [per_device(): lax.psum_scatter(lax.dot_general(received, hidden, (((0,), (0,)), ((), ()...]
    all_to_all x2 -> x0, starting transfers between devices: 31.4 us -> none  [the longest x1 19.4 us: per_device(): lax.all_to_all(outgoing, 'expert', split_axis=0, concat_axis=0, tiled=True)]
    dot_general x9 -> x0, matrix products: 31 us -> none  [the longest x2 10.5 us: add_rows(): return jnp.dot(arrived, piece, preferred_element_type=jnp.float32)]
    reshape x3 -> x0, local copies, waits for them, and re-layouts: 9.63 us -> none  [the longest x1 3.45 us: per_device(): lax.all_to_all(sending, 'expert', split_axis=0, concat_axis=0, tiled=True)]
  transfers between devices with their start and end apart: 6 -> 0, of which waited for: 3 -> 0; matrix products, arithmetic and copies ran while one was open for 3% -> 0% of each run, Pallas kernels for 0% -> 0%
where the time goes in v2:
time: 211 us
  Pallas kernels  205 us (97%)
  local copies, waits for them, and re-layouts  4.19 us (2%)
    pallas_call x1, Pallas kernels, per_device(): pl.pallas_call(kernel, out_shape=(jax.ShapeDtypeStruct((tokens, width), F...  205 us

profile of v2, /device:TPU:1, one launch (start us, length us, event | category | flops | bytes accessed | tf_op | source)
XLA Modules:
  0.0 210.7 jit_solution(10303349920544304280)
XLA Ops:
  0.6 0.0 copy-start.1
  0.6 0.7 copy-done.1
  1.3 0.0 copy-start.2
  1.3 0.7 copy-done.2
  2.0 0.7 maximum_maximum_fusion.tab_ref
  2.7 205.1 %shard_map.86 = (f32[64,2048]{1,0:T(8,128)}, f32[256,768]{1,0:T(8,128)}) custom-call(bf16[64,2048]{1,0:T(8,128)(2,1)} %tok_ref.1, bf16[64,2048]{1,0:T(8,128)(2,1)} %curv_ref.1, f32[16,128]{1,0:T(8,128)} %maximum_maximum_fusion.tab_ref, bf16[256,768]{1,0:T(8,128)(2,1)} %bitcast.8, bf16[256,768]{1,0:T(8,128)(2,1)} %bitcast.9, bf16[256,768]{1,0:T(8,128)(2,1)} %bitcast.10), custom_call_target="tpu_custom_call" | custom-call | tf_op jit(solution)/shard_map/pallas_call | solution.py:419
  207.8 0.0 copy-start
  207.8 1.9 copy.11
  209.8 0.0 copy-done
  209.8 0.9 copy.12
  (1 shorter events, 0.0 us)
Async XLA Ops:
  0.6 0.7 copy-start.1
  1.3 0.7 copy-start.2
  207.8 2.0 copy-start

commit v3 on v2

--- a/solution.py
+++ b/solution.py
@@ -14,11 +14,31 @@
 CAP = 9
 CHUNKS = 4
 PAIR = 2 * TOK
-GROUPS = ((1, 2, 3), (4, 5, 6), (7, 0))
-ROWS = tuple(-(-len(g) * 2 * CAP // 16) * 16 for g in GROUPS)
+OWN, FAR = 0, HALF
+BOUNDS = (0, 48, 80, 112, 128, 144)
+
+
+def many(k):
+    return 1 if k in (OWN, FAR) else 2
+
+
+def first_row(k):
+    return 0 if k == OWN else CAP * (2 * k - 1)
+
+
+GROUPS = tuple(
+    tuple(
+        k
+        for k in range(HALF + 1)
+        if first_row(k) < hi and first_row(k) + CAP * many(k) > lo
+    )
+    for lo, hi in zip(BOUNDS, BOUNDS[1:])
+)
+COLS = tuple(TOK * sum(many(k) for k in g) for g in GROUPS)
+ROWS = tuple(hi - lo for lo, hi in zip(BOUNDS, BOUNDS[1:]))
 STARTS = tuple(X * sum(ROWS[:g]) for g in range(len(GROUPS)))
 TOTAL = X * sum(ROWS)
-LAG = 1
+LAG = 2
 MESH = pl.DeviceIdType.MESH
 F32 = jnp.float32
 BF16 = jnp.bfloat16
@@ -30,12 +50,14 @@
 
 def kernel(
     tok_ref, curv_ref, tab_ref, wg_ref, wu_ref, wd_ref, tan_ref, out_ref,
-    wf, zb1, tb, qs, ws, pm0, pm1, pm2, gm0, gm1, gm2, gt0, gt1, gt2,
-    st1, arr, hid, st2, br, rs_s, rs_r, sc, zb3, st3, rr, own, ps, pr, ys, yr,
-    w_loc, w_ss, w_rs, f_ss, f_rs, z1_s, z1_r, t_s, t_r, x1_s, x1_r, x2_s, x2_r,
+    wf, zb1, tb, qs, ws, pm0, pm1, pm2, pm3, pm4, gm0, gm1, gm2, gm3, gm4, gt0, gt1, gt2, gt3, gt4,
+    st1, arr, hid, st2, br, rs_s, rs_r, sc, zb3, st3, rr, own, ps, pr, ys, yr, half, tok_v, curv_v,
+    in_s, w_loc, w_ss, w_rs, r_ss, r_rs, f_ss, f_rs, z1_s, z1_r, t_s, t_r, x1_s, x1_r, x2_s, x2_r,
     rs_ss, rs_rs, z3_s, z3_r, x3_s, x3_r, p_s, p_r, y_s, y_r,
 ):
-    pm, gm, gt = (pm0, pm1, pm2), (gm0, gm1, gm2), (gt0, gt1, gt2)
+    pm = (pm0, pm1, pm2, pm3, pm4)
+    gm = (gm0, gm1, gm2, gm3, gm4)
+    gt = (gt0, gt1, gt2, gt3, gt4)
     dp = lax.axis_index("dp")
     e = lax.axis_index("expert")
     zi, xi = e // X, lax.rem(e, X)
@@ -66,14 +88,22 @@
         copy.start()
         sends.append(copy)
 
+    loads = [
+        pltpu.make_async_copy(tok_ref, tok_v, in_s.at[0]),
+        pltpu.make_async_copy(curv_ref, curv_v, in_s.at[1]),
+    ]
+    for load in loads:
+        load.start()
     barrier = pltpu.get_barrier_semaphore()
     partners = [at_z(1), at_z(-1), at_x(1), at_x(2), at_x(3), at_y(1), at_y(2), at_y(3), sibling]
     for dev in partners:
         pl.semaphore_signal(barrier, inc=1, device_id=dev, device_id_type=MESH)
     pl.semaphore_wait(barrier, len(partners))
+    for load in loads:
+        load.wait()
 
     def z1_copy(d, k, j):
-        src = tok_ref.at[:, j * cw : (j + 1) * cw] if k == 0 else zb1.at[d, k - 1, j]
+        src = tok_v.at[:, j * cw : (j + 1) * cw] if k == 0 else zb1.at[d, k - 1, j]
         return remote(src, zb1.at[d, k, j], z1_s.at[d, k, j], z1_r.at[d, k, j], at_z(1 - 2 * d))
 
     def t_copy(d, k):
@@ -95,8 +125,9 @@
     def block(g, r):
         return slice(STARTS[g] + r * ROWS[g], STARTS[g] + (r + 1) * ROWS[g])
 
-    def group(g):
-        return slice(STARTS[g], STARTS[g] + X * ROWS[g])
+    def group(g, last=None):
+        last = g if last is None else last
+        return slice(STARTS[g], STARTS[last] + X * ROWS[last])
 
     def x1_copy(g, r):
         rows = block(g, r)
@@ -119,7 +150,15 @@
 
     def w_copy(m, r):
         return remote(
-            w_refs[m], wf.at[m, wrows(yi)], w_ss.at[m, r - 1], w_rs.at[m, r - 1], at_y(r)
+            w_refs[m], wf.at[m, wrows(yi)], w_ss.at[m, r // 2], w_rs.at[m, r // 2], at_y(r)
+        )
+
+    def relay_copy(m, h):
+        y = lax.rem(yi + Y - 1 + 2 * h, Y)
+        start = (y * 2 + ci) * drows + h * (drows // 2)
+        rows = pl.ds(pl.multiple_of(start, drows // 2), drows // 2)
+        return remote(
+            wf.at[m, rows], wf.at[m, rows], r_ss.at[m, h], r_rs.at[m, h], at_y(1 - 2 * h)
         )
 
     def f_copy(m, r):
@@ -131,10 +170,17 @@
     def w_local(m):
         return pltpu.make_async_copy(w_refs[m], wf.at[m, wrows(yi)], w_loc.at[m])
 
+    def relay_weight(m):
+        for h, r in enumerate((1, 3)):
+            w_copy(m, r).wait_recv()
+            go(relay_copy(m, h))
+        for r in (1, 3):
+            go(f_copy(m, r))
+
     def share_weight(m):
-        for r in (1, 3, 2):
-            w_copy(m, r).wait_recv()
-            go(f_copy(m, r))
+        for h in range(2):
+            relay_copy(m, h).wait_recv()
+        go(f_copy(m, 2))
 
     def finish_weight(m):
         w_local(m).wait()
@@ -147,13 +193,19 @@
     before = (upper_row < upper_col) & ((upper_row < TOK) == (upper_col < TOK))
     before = before.astype(F32).astype(BF16)
 
-    def route(k, spot):
-        if k == 0:
-            first, second = tab_ref[...], tb[0, HALF - 1]
-        else:
+    def spot(g, k):
+        members = GROUPS[g]
+        start = TOK * sum(many(m) for m in members[: members.index(k)])
+        return slice(start, start + many(k) * TOK)
+
+    def route(k):
+        first = second = tab_ref[...]
+        if k == FAR:
+            first = tb[0, HALF - 1]
+        elif k != OWN:
             first, second = tb[0, k - 1], tb[1, k - 1]
-        table = jnp.where(lane < TOK, first, second)
-        gates, names = table[:8], table[8:]
+        gates = jnp.where(lane < TOK, first, pltpu.roll(second, TOK, axis=1))
+        names = jnp.where(lane < TOK, pltpu.roll(first, TOK, axis=1), second)
         count, weight = [], []
         for r in range(X):
             expert = (zi * X + lax.rem(xi + r, X)).astype(F32)
@@ -163,29 +215,31 @@
         fill = jnp.zeros((8 - X, PAIR), F32)
         count = jnp.concatenate(count + [fill], axis=0)
         slot = dot(count.astype(BF16), before)
-        base = jnp.where(lane < TOK, 2 * CAP * spot, 2 * CAP * spot + CAP).astype(F32)
+        base = jnp.where(lane < TOK, first_row(k), first_row(k) + CAP).astype(F32)
         qs[k] = jnp.where(count > 0.0, slot + base, -1.0)
         ws[k] = jnp.concatenate(weight + [fill], axis=0)
 
     def tables(g):
         rows = ROWS[g]
-        for spot, k in enumerate(GROUPS[g]):
-            cols = slice(spot * PAIR, (spot + 1) * PAIR)
-            number = lax.broadcasted_iota(jnp.int32, (rows, PAIR), 0).astype(F32)
+        number = (lax.broadcasted_iota(jnp.int32, (rows, PAIR), 0) + BOUNDS[g]).astype(F32)
+        for k in GROUPS[g]:
+            cols, size = spot(g, k), many(k) * TOK
             parts = []
             for r in range(X):
                 hit = number == qs[k][r : r + 1]
                 here = slice(r * rows, (r + 1) * rows)
-                pm[g][here, cols] = jnp.where(hit, 1.0, 0.0).astype(BF16)
+                pm[g][here, cols] = jnp.where(hit, 1.0, 0.0).astype(BF16)[:, :size]
                 weighted = jnp.where(hit, ws[k][r : r + 1], 0.0)
-                gm[g][here, cols] = weighted.astype(BF16)
+                gm[g][here, cols] = weighted.astype(BF16)[:, :size]
                 parts.append(weighted)
-            gt[g][cols, :] = jnp.concatenate(parts, axis=0).T.astype(BF16)
+            gt[g][cols, :] = jnp.concatenate(parts, axis=0).T.astype(BF16)[:size]
 
     def tokens_of(k, j):
         cols = slice(j * cw, (j + 1) * cw)
-        if k == 0:
-            return [tok_ref[:, cols], zb1[0 if j < CHUNKS // 2 else 1, HALF - 1, j]]
+        if k == OWN:
+            return [tok_v[:, cols]]
+        if k == FAR:
+            return [zb1[0 if j < CHUNKS // 2 else 1, HALF - 1, j]]
         return [zb1[0, k - 1, j], zb1[1, k - 1, j]]
 
     def select(g):
@@ -198,15 +252,16 @@
         for r in (2, 1, 3):
             go(x1_copy(g, r))
 
-    def hide(g):
-        for r in (2, 1, 3):
-            x1_copy(g, r).wait_recv()
+    def hide(g, last):
+        for n in range(g, last + 1):
+            for r in (2, 1, 3):
+                x1_copy(n, r).wait_recv()
 
         def tile(n, _):
             cols = pl.ds(pl.multiple_of(n * 256, 256), 256)
-            gate = dot(arr[group(g), :], wf[0, :, cols])
-            up = dot(arr[group(g), :], wf[1, :, cols])
-            hid[group(g), cols] = (gate / (1.0 + jnp.exp(-gate)) * up).astype(BF16)
+            gate = dot(arr[group(g, last), :], wf[0, :, cols])
+            up = dot(arr[group(g, last), :], wf[1, :, cols])
+            hid[group(g, last), cols] = (gate / (1.0 + jnp.exp(-gate)) * up).astype(BF16)
             return 0
 
         lax.fori_loop(0, hid.shape[1] // 256, tile, 0)
@@ -219,10 +274,11 @@
                 go(t_copy(d, 0))
             go(z1_copy(d, 0, j))
     for m in range(3):
-        for r in (1, 3, 2):
+        for r in (1, 3):
             go(w_copy(m, r))
         go(f_copy(m, 0))
 
+    route(OWN)
     for k in range(1, HALF + 1):
         for j in range(CHUNKS):
             for d in range(2):
@@ -234,56 +290,57 @@
                     z1_copy(d, k - 1, j).wait_recv()
                 if k < HALF and live(d, k, j):
                     go(z1_copy(d, k, j))
-        pair = k % HALF
+        route(k)
         for g, members in enumerate(GROUPS):
-            if pair in members:
-                route(pair, members.index(pair))
-                if pair == members[-1]:
-                    tables(g)
-                    select(g)
-        if k == 4:
-            share_weight(0)
-        if k == 7:
-            share_weight(1)
-            finish_weight(0)
-            finish_weight(1)
-            hide(0)
-    hide(1)
+            if k == max(members):
+                tables(g)
+                select(g)
+        if k in (2, 3, 5):
+            relay_weight({2: 0, 3: 1, 5: 2}[k])
+        if k in (5, 6):
+            share_weight(k - 5)
+    finish_weight(0)
+    finish_weight(1)
+    hide(0, 2)
     share_weight(2)
-    hide(2)
+    hide(3, 4)
     finish_weight(2)
 
     def place(i):
         return lax.rem(yi + 1 + i, CHUNKS)
 
-    def back(g, i):
+    def back(g, last, i):
         rows = pl.ds(pl.multiple_of(place(i) * cw, cw), cw)
-        made = dot(hid[group(g), :], wf[2, rows, :], ((1,), (1,))).astype(BF16)
-        br[i, block(g, 0)] = made[: ROWS[g]]
-        st2[i, STARTS[g] + ROWS[g] : STARTS[g] + X * ROWS[g]] = made[ROWS[g] :]
-        for r in (2, 1, 3):
-            go(x2_copy(g, i, r))
+        made = dot(hid[group(g, last), :], wf[2, rows, :], ((1,), (1,))).astype(BF16)
+        for n in range(last, g - 1, -1):
+            start = STARTS[n] - STARTS[g]
+            br[i, block(n, 0)] = made[start : start + ROWS[n]]
+            rest = slice(STARTS[n] + ROWS[n], STARTS[n] + X * ROWS[n])
+            st2[i, rest] = made[start + ROWS[n] : start + X * ROWS[n]]
+            for r in (2, 1, 3):
+                go(x2_copy(n, i, r))
+
+    arrived = set()
 
     def share(k, i):
+        total = None
         for g, members in enumerate(GROUPS):
             if k in members:
-                spot = members.index(k)
-                return dot(gt[g][spot * PAIR : (spot + 1) * PAIR, :], br[i, group(g)])
-
-    order = len(GROUPS) - 1
+                if (g, i) not in arrived:
+                    arrived.add((g, i))
+                    for r in (2, 1, 3):
+                        x2_copy(g, i, r).wait_recv()
+                part = dot(gt[g][spot(g, k), :], br[i, group(g)])
+                total = part if total is None else total + part
+        return total
 
     def reduce_step(i, s):
-        if s in (0, 2, 5):
-            g = {0: 2, 2: 1, 5: 0}[s]
-            for r in (2, 1, 3):
-                x2_copy(g, i, r).wait_recv()
-        part = share((HALF - s) % HALF, i)
+        part = share(HALF - s, i)
         if s == 0:
             d = 0 if i < CHUNKS // 2 else 1
-            rs_s[d, 0, i] = part[TOK:].astype(BF16)
+            rs_s[d, 0, i] = part.astype(BF16)
             go(rs_copy(d, 0, i))
-            own[i] = part[:TOK]
-            back(1, i)
+            back(2, 2, i)
         else:
             for d in range(2):
                 mine = part[TOK:] if d == 0 else part[:TOK]
@@ -292,8 +349,10 @@
                     mine = mine + rs_r[d, s - 1, i].astype(F32)
                 rs_s[d, s, i] = mine.astype(BF16)
                 go(rs_copy(d, s, i))
-            if s == 1:
-                back(0, i)
+            if s in (1, 2):
+                back(2 - s, 2 - s, i)
+            if s == 6:
+                own[i] = share(OWN, i)
 
     def finish_tangent(i):
         cols = pl.ds(pl.multiple_of(place(i) * cw, cw), cw)
@@ -302,13 +361,15 @@
             rs_copy(d, HALF - 1, i).wait_recv()
             total = total + rs_r[d, HALF - 1, i].astype(F32)
         tan_ref[:, cols] = total
-        sc[i] = (curv_ref[:, cols].astype(F32) * total).astype(BF16)
+        sc[i] = (curv_v[:, cols].astype(F32) * total).astype(BF16)
         for d in range(2):
             go(z3_copy(d, 0, i))
 
     def scaled_of(k, i):
-        if k == 0:
-            return [sc[i], zb3[0 if i < CHUNKS // 2 else 1, HALF - 1, i]]
+        if k == OWN:
+            return [sc[i]]
+        if k == FAR:
+            return [zb3[0 if i < CHUNKS // 2 else 1, HALF - 1, i]]
         return [zb3[0, k - 1, i], zb3[1, k - 1, i]]
 
     def gather_step(i, k):
@@ -318,7 +379,7 @@
             if k < HALF and live(d, k, i):
                 go(z3_copy(d, k, i))
         for g, members in enumerate(GROUPS):
-            if k % HALF == members[-1]:
+            if k == max(members):
                 source = jnp.concatenate([t for m in members for t in scaled_of(m, i)], axis=0)
                 picked = dot(gm[g][...], source).astype(BF16)
                 rr[i, block(g, 0)] = picked[: ROWS[g]]
@@ -327,7 +388,12 @@
                     go(x3_copy(g, i, r))
 
     hw = cw // 2
-    held = []
+
+    def pair_copy(i):
+        return remote(ps.at[i], pr.at[i], p_s.at[i], p_r.at[i], sibling)
+
+    def home_copy(i):
+        return remote(ys.at[i], yr.at[i], y_s.at[i], y_r.at[i], at_y(1 + i))
 
     def multiply(i):
         for g in range(len(GROUPS)):
@@ -336,22 +402,24 @@
         theirs = pl.ds(pl.multiple_of((1 - ci) * hw, hw), hw)
         mine = pl.ds(pl.multiple_of(ci * hw, hw), hw)
         ps[i] = dot(rr[i, :, theirs], hid[...], ((0,), (0,))).astype(BF16)
-        go(remote(ps.at[i], pr.at[i], p_s.at[i], p_r.at[i], sibling))
-        out_ref[...] = dot(rr[i, :, mine], hid[...], ((0,), (0,)))
-        remote(ps.at[i], pr.at[i], p_s.at[i], p_r.at[i], sibling).wait_recv()
-        total = out_ref[...] + pr[i].astype(F32)
+        go(pair_copy(i))
+        half[i % 2] = dot(rr[i, :, mine], hid[...], ((0,), (0,)))
+
+    def send_home(i):
+        pair_copy(i).wait_recv()
+        total = half[i % 2] + pr[i].astype(F32)
         if i < Y - 1:
             ys[i] = total.astype(BF16)
-            go(remote(ys.at[i], yr.at[i], y_s.at[i], y_r.at[i], at_y(1 + i)))
+            go(home_copy(i))
         else:
             for n in range(Y - 1):
-                remote(ys.at[n], yr.at[n], y_s.at[n], y_r.at[n], at_y(1 + n)).wait_recv()
+                home_copy(n).wait_recv()
                 total = total + yr[n].astype(F32)
             out_ref[...] = total
 
     for i in range(CHUNKS):
-        back(2, i)
-    for tick in range(2 * HALF + 2 + LAG * (CHUNKS - 1)):
+        back(3, 4, i)
+    for tick in range(2 * HALF + 3 + LAG * (CHUNKS - 1)):
         for i in range(CHUNKS):
             u = tick - LAG * i
             if 0 <= u < HALF:
@@ -362,6 +430,8 @@
                 gather_step(i, u - HALF)
             elif u == 2 * HALF + 1:
                 multiply(i)
+            elif u == 2 * HALF + 2:
+                send_home(i)
 
     for copy in sends:
         copy.wait_send()
@@ -371,8 +441,7 @@
     tokens, width = activations.shape
     features, hidden = w_gate.shape[1:]
     cw = width // CHUNKS
-    table = jnp.concatenate([route_gates.T, routes.T.astype(F32)], axis=0)
-    table = jnp.concatenate([table, table], axis=1)
+    table = jnp.concatenate([route_gates.T, routes.T.astype(F32)], axis=1)
     vmem = pl.BlockSpec(memory_space=pltpu.VMEM)
     hbm = pl.BlockSpec(memory_space=pl.ANY)
     dma = pltpu.SemaphoreType.DMA
@@ -381,11 +450,11 @@
         pltpu.VMEM((3, width, hidden), BF16),
         pltpu.VMEM((2, HALF, CHUNKS, tokens, cw), BF16),
         pltpu.VMEM((2, HALF) + table.shape, F32),
-        pltpu.VMEM((HALF, 8, PAIR), F32),
-        pltpu.VMEM((HALF, 8, PAIR), F32),
+        pltpu.VMEM((HALF + 1, 8, PAIR), F32),
+        pltpu.VMEM((HALF + 1, 8, PAIR), F32),
     ]
-    scratch += [pltpu.VMEM((X * ROWS[g], PAIR * len(GROUPS[g])), BF16) for g in range(n)] * 2
-    scratch += [pltpu.VMEM((PAIR * len(GROUPS[g]), X * ROWS[g]), BF16) for g in range(n)]
+    scratch += [pltpu.VMEM((X * ROWS[g], COLS[g]), BF16) for g in range(n)] * 2
+    scratch += [pltpu.VMEM((COLS[g], X * ROWS[g]), BF16) for g in range(n)]
     scratch += [
         pltpu.VMEM((TOTAL, width), BF16),
         pltpu.VMEM((TOTAL, width), BF16),
@@ -403,8 +472,13 @@
         pltpu.VMEM((CHUNKS, features, hidden), BF16),
         pltpu.VMEM((Y - 1, features, hidden), BF16),
         pltpu.VMEM((Y - 1, features, hidden), BF16),
+        pltpu.VMEM((2, features, hidden), F32),
+        pltpu.VMEM((tokens, width), BF16),
+        pltpu.VMEM((tokens, width), BF16),
+        dma((2,)),
         dma((3,)),
-        dma((3, Y - 1)), dma((3, Y - 1)),
+        dma((3, 2)), dma((3, 2)),
+        dma((3, 2)), dma((3, 2)),
         dma((3, Y)), dma((3, Y)),
         dma((2, HALF, CHUNKS)), dma((2, HALF, CHUNKS)),
         dma((2, HALF)), dma((2, HALF)),
@@ -422,7 +496,7 @@
             jax.ShapeDtypeStruct((tokens, width), F32),
             jax.ShapeDtypeStruct((features, hidden), F32),
         ),
-        in_specs=[vmem, vmem, vmem, hbm, hbm, hbm],
+        in_specs=[hbm, hbm, vmem, hbm, hbm, hbm],
         out_specs=(vmem, vmem),
         scratch_shapes=scratch,
         compiler_params=pltpu.CompilerParams(

time: 211 us -> 199 us (0.943)
  Pallas kernels: 205 us -> 193 us
    pallas_call x1, Pallas kernels: 205 us -> 193 us  [per_device(): pl.pallas_call(kernel, out_shape=(jax.ShapeDtypeStruct((tokens, width), F...]
where the time goes in v3:
time: 199 us
  Pallas kernels  193 us (97%)
  local copies, waits for them, and re-layouts  4.19 us (2%)
    pallas_call x1, Pallas kernels, per_device(): pl.pallas_call(kernel, out_shape=(jax.ShapeDtypeStruct((tokens, width), F...  193 us
    unnamed x8, local copies, waits for them, and re-layouts  4.19 us

profile of v3, /device:TPU:1, one launch (start us, length us, event | category | flops | bytes accessed | tf_op | source)
XLA Modules:
  0.0 198.5 jit_solution(12418129055656962916)
XLA Ops:
  0.6 0.0 copy-start.2
  0.6 0.7 copy-done.2
  1.3 0.0 copy-start.1
  1.3 0.7 copy-done.1
  2.0 0.7 pad_maximum_fusion.tab_ref
  2.7 193.0 %shard_map.86 = (f32[64,2048]{1,0:T(8,128)}, f32[256,768]{1,0:T(8,128)}) custom-call(bf16[64,2048]{1,0:T(8,128)(2,1)} %tok_ref.1, bf16[64,2048]{1,0:T(8,128)(2,1)} %curv_ref.1, f32[8,128]{1,0:T(8,128)} %pad_maximum_fusion.tab_ref, bf16[256,768]{1,0:T(8,128)(2,1)} %bitcast.8, bf16[256,768]{1,0:T(8,128)(2,1)} %bitcast.9, bf16[256,768]{1,0:T(8,128)(2,1)} %bitcast.10), custom_call_target="tpu_custom_call" | custom-call | tf_op jit(solution)/shard_map/pallas_call | solution.py:493
  195.7 0.0 copy-start
  195.7 1.9 copy.11
  197.7 0.0 copy-done
  197.7 0.9 copy.12
  (1 shorter events, 0.0 us)
Async XLA Ops:
  0.6 0.7 copy-start.2
  1.3 0.7 copy-start.1
  195.7 2.0 copy-start

commit v4 on v3

--- a/solution.py
+++ b/solution.py
@@ -417,7 +417,7 @@
                 total = total + yr[n].astype(F32)
             out_ref[...] = total
 
-    for i in range(CHUNKS):
+    for i in range(2):
         back(3, 4, i)
     for tick in range(2 * HALF + 3 + LAG * (CHUNKS - 1)):
         for i in range(CHUNKS):
@@ -432,6 +432,8 @@
                 multiply(i)
             elif u == 2 * HALF + 2:
                 send_home(i)
+        if tick < CHUNKS - 2:
+            back(3, 4, 2 + tick)
 
     for copy in sends:
         copy.wait_send()

time: 199 us -> 198 us (level)
  no operation moved by 1% of the time
where the time goes in v4:
time: 198 us
  Pallas kernels  192 us (97%)
  local copies, waits for them, and re-layouts  4.19 us (2%)
    pallas_call x1, Pallas kernels, per_device(): pl.pallas_call(kernel, out_shape=(jax.ShapeDtypeStruct((tokens, width), F...  192 us
    unnamed x8, local copies, waits for them, and re-layouts  4.19 us

profile of v4, /device:TPU:1, one launch (start us, length us, event | category | flops | bytes accessed | tf_op | source)
XLA Modules:
  0.0 198.0 jit_solution(8970206379449222936)
XLA Ops:
  0.6 0.0 copy-start.2
  0.6 0.7 copy-done.2
  1.3 0.0 copy-start.1
  1.3 0.7 copy-done.1
  2.0 0.7 pad_maximum_fusion.tab_ref
  2.7 192.5 %shard_map.86 = (f32[64,2048]{1,0:T(8,128)}, f32[256,768]{1,0:T(8,128)}) custom-call(bf16[64,2048]{1,0:T(8,128)(2,1)} %tok_ref.1, bf16[64,2048]{1,0:T(8,128)(2,1)} %curv_ref.1, f32[8,128]{1,0:T(8,128)} %pad_maximum_fusion.tab_ref, bf16[256,768]{1,0:T(8,128)(2,1)} %bitcast.8, bf16[256,768]{1,0:T(8,128)(2,1)} %bitcast.9, bf16[256,768]{1,0:T(8,128)(2,1)} %bitcast.10), custom_call_target="tpu_custom_call" | custom-call | tf_op jit(solution)/shard_map/pallas_call | solution.py:495
  195.2 0.0 copy-start
  195.2 1.9 copy.11
  197.1 0.0 copy-done
  197.1 0.9 copy.12
  (1 shorter events, 0.0 us)
Async XLA Ops:
  0.6 0.7 copy-start.2
  1.3 0.7 copy-start.1
  195.2 2.0 copy-start
